TPU v7x, 128 devices: a whole 4x4x4 slice. The times are simulated.
128 devices in a mesh: tile: 16 (over z, y), seq: 8 (over x, core).
Axes of the slice: x: 4, y: 4, z: 4, core: 2. Of those that a mesh axis runs over, the one named last changes fastest.
Arguments:
- cls_tokens: bfloat16 [16384, 1536], P(('tile', 'seq')), may hold values from -6 to 6
- norm_gain: float32 [1536], replicated, may hold values from 0.5 to 1.5
- w_gate: bfloat16 [1536, 4096], P(None, 'tile'), may hold values from -0.15625 to 0.15625
- w_up: bfloat16 [1536, 4096], P(None, 'tile'), may hold values from -0.15625 to 0.15625
- w_down: bfloat16 [4096, 1536], P('tile'), may hold values from -0.09375 to 0.09375
- layer_scale: float32 [1536], replicated, may hold values from 0.25 to 1.75
- final_gain: float32 [1536], replicated, may hold values from 0.5 to 1.5
- w_embed: bfloat16 [1536, 768], replicated, may hold values from -0.15625 to 0.15625
- dest_pos: int32 [16384], P(('tile', 'seq')), may hold values from 0 to 16383, as said below
- tile_coords: int32 [2, 16384], P(None, ('tile', 'seq')), may hold values from 0 to 999
- attn_gain: float32 [768], replicated, may hold values from 0.5 to 1.5
- w_qkv: bfloat16 [768, 2304], replicated, may hold values from -4 to 4
- offsets: int32 [12], replicated, may hold values from 0 to 15
- w_out: bfloat16 [768, 768], replicated, may hold values from -0.21875 to 0.21875
Outputs:
- slide_out: bfloat16 [16384, 768], P(('tile', 'seq'))
Inputs may be any that keep to these rules, and one draw needn't show every extreme that they name: dest_pos holds each number of 0 to 16383 once; the 128 rows of one device go to the devices of the slide order in groups of 0, 1 or 2 rows a device, some pair carrying 2; every device receives 128 rows, 2 of them from the device 128 / 2 places before it in the slide order, counted round.
All inputs are finite; a program needn't handle non-finite values.
Results may differ from a plain program's by a relative error of at most 0.018.
Values may be sent and summed in bfloat16 or wider, within the bound.
No kernel may reach another device: no remote copies, remote signals or barrier semaphores. Data moves between devices by JAX's collectives and lax.ppermute only.
A program may use at most 128 MiB of HBM per device.

v0:
```python
import jax
import jax.numpy as jnp
from jax import lax
from jax.sharding import PartitionSpec as P

HEAD_COUNT = 12
HEAD_WIDTH = 64
SEGMENT_SPACING = 16


def layer_norm(sender_rows, gain):
    average = jnp.mean(sender_rows, axis=-1, keepdims=True)
    centered = sender_rows - average
    variance = jnp.mean(centered * centered, axis=-1, keepdims=True)
    return centered * lax.rsqrt(variance + 1e-06) * gain


def position_table(coords, hidden_width):
    quarter = hidden_width // 4
    frequency = 1.0 / 10000.0 ** (jnp.arange(quarter).astype(jnp.float32) / quarter)
    along_x = coords[:, 0:1].astype(jnp.float32) * frequency[None, :]
    along_y = coords[:, 1:2].astype(jnp.float32) * frequency[None, :]
    return jnp.concatenate(
        [jnp.sin(along_x), jnp.cos(along_x), jnp.sin(along_y), jnp.cos(along_y)], axis=1
    )


def attend(queries, key_rows, values):
    score_scale = queries.shape[-1] ** (-0.5)
    scores = (
        jnp.einsum("qhd,khd->hqk", queries, key_rows, preferred_element_type=jnp.float32)
        * score_scale
    )
    highest = jnp.max(scores, axis=-1, keepdims=True)
    weights = jnp.exp(scores - highest)
    totals = jnp.sum(weights, axis=-1, keepdims=True)
    mixed_rows = jnp.einsum(
        "hqk,khd->qhd", weights.astype(jnp.bfloat16), values, preferred_element_type=jnp.float32
    )
    result = mixed_rows / jnp.transpose(totals, (1, 0, 2))
    logsum = jnp.transpose((highest + jnp.log(totals))[:, :, 0])
    return (result, logsum)


def body(
    cls_tokens,
    norm_gain,
    w_gate,
    w_up,
    w_down,
    layer_scale,
    final_gain,
    w_embed,
    dest_pos,
    tile_coords,
    attn_gain,
    w_qkv,
    offsets,
    w_out,
):
    resident_rows = cls_tokens.shape[0]
    tokens = cls_tokens.astype(jnp.float32)
    normed = layer_norm(tokens, norm_gain).astype(jnp.bfloat16)
    shard_rows = lax.all_gather(normed, "tile", axis=0, tiled=True)
    gate_proj = jnp.dot(shard_rows, w_gate, preferred_element_type=jnp.float32)
    upward = jnp.dot(shard_rows, w_up, preferred_element_type=jnp.float32)
    hidden = (jax.nn.silu(gate_proj) * upward).astype(jnp.bfloat16)
    projected = lax.psum_scatter(
        jnp.dot(hidden, w_down, preferred_element_type=jnp.float32),
        "tile",
        scatter_dimension=0,
        tiled=True,
    )
    mixed_rows = tokens + layer_scale * projected
    final_rows = layer_norm(mixed_rows, final_gain).astype(jnp.bfloat16)
    embedded = jnp.dot(final_rows, w_embed, preferred_element_type=jnp.float32).astype(jnp.bfloat16)
    hidden_width = embedded.shape[1]
    tile_count = lax.axis_size("tile")
    seq_count = lax.axis_size("seq")
    devices = tile_count * seq_count
    capacity = 2 * max(1, resident_rows // devices)
    target = dest_pos // resident_rows
    row_ids = jnp.arange(resident_rows)
    earlier = (target[:, None] == target[None, :]) & (row_ids[None, :] < row_ids[:, None])
    slot_index = jnp.sum(earlier.astype(jnp.int32), axis=1)
    where_to = target * capacity + slot_index
    payload = jnp.zeros((devices * capacity, hidden_width), jnp.bfloat16).at[where_to].set(embedded)
    meta_rows = jnp.stack([dest_pos, tile_coords[0], tile_coords[1]], axis=1)
    meta_table = jnp.full((devices * capacity, 3), -1, jnp.int32).at[where_to].set(meta_rows)
    received, received_meta = (
        lax.all_to_all(
            payload.reshape(devices, capacity, hidden_width),
            ("tile", "seq"),
            split_axis=0,
            concat_axis=0,
            tiled=True,
        ),
        lax.all_to_all(
            meta_table.reshape(devices, capacity, 3),
            ("tile", "seq"),
            split_axis=0,
            concat_axis=0,
            tiled=True,
        ),
    )
    flat_rows = received.reshape(-1, hidden_width)
    flat_meta = received_meta.reshape(-1, 3)
    is_live = flat_meta[:, 0] >= 0
    local_slot = jnp.where(is_live, flat_meta[:, 0] % resident_rows, resident_rows)
    placed = (
        jnp.zeros((resident_rows, hidden_width), jnp.bfloat16)
        .at[local_slot]
        .set(flat_rows, mode="drop")
    )
    coords = (
        jnp.zeros((resident_rows, 2), jnp.int32).at[local_slot].set(flat_meta[:, 1:], mode="drop")
    )
    seq_in = placed.astype(jnp.float32) + position_table(coords, hidden_width)
    normed_seq = layer_norm(seq_in, attn_gain).astype(jnp.bfloat16)
    qkv = jnp.dot(normed_seq, w_qkv, preferred_element_type=jnp.float32).astype(jnp.bfloat16)
    queries = qkv[:, :hidden_width]
    keys_values = qkv[:, hidden_width:]
    segment_kv = lax.all_gather(keys_values, "seq", axis=0, tiled=True)
    near_out, nearby_logsumexp = attend(
        queries.reshape(resident_rows, HEAD_COUNT, HEAD_WIDTH),
        segment_kv[:, :hidden_width].reshape(-1, HEAD_COUNT, HEAD_WIDTH),
        segment_kv[:, hidden_width:].reshape(-1, HEAD_COUNT, HEAD_WIDTH),
    )
    kept_rows = jnp.arange(SEGMENT_SPACING, dtype=jnp.int32)[:, None] == offsets[None, :]

    def select(sender_rows, stacked_rows):
        head_grouped = sender_rows.reshape(
            resident_rows // SEGMENT_SPACING, SEGMENT_SPACING, stacked_rows, HEAD_COUNT, HEAD_WIDTH
        )
        sampled_rows = jnp.sum(
            jnp.where(
                kept_rows[None, :, None, :, None], head_grouped, jnp.zeros((), sender_rows.dtype)
            ),
            axis=1,
        )
        return sampled_rows.reshape(resident_rows // SEGMENT_SPACING, stacked_rows * hidden_width)

    far_kv = lax.all_gather(select(keys_values, 2), ("tile", "seq"), axis=0, tiled=True)
    far_out, far_lse = attend(
        select(queries, 1).reshape(-1, HEAD_COUNT, HEAD_WIDTH),
        far_kv[:, :hidden_width].reshape(-1, HEAD_COUNT, HEAD_WIDTH),
        far_kv[:, hidden_width:].reshape(-1, HEAD_COUNT, HEAD_WIDTH),
    )
    far_full = jnp.where(kept_rows[None, :, :, None], far_out[:, None], 0.0).reshape(
        resident_rows, HEAD_COUNT, HEAD_WIDTH
    )
    nearby_grouped = nearby_logsumexp.reshape(
        resident_rows // SEGMENT_SPACING, SEGMENT_SPACING, HEAD_COUNT
    )
    far_share = jnp.where(
        kept_rows[None], 1.0 / (1.0 + jnp.exp(nearby_grouped - far_lse[:, None])), 0.0
    ).reshape(resident_rows, HEAD_COUNT)
    combined = (1.0 - far_share)[:, :, None] * near_out + far_share[:, :, None] * far_full
    attn_rows = combined.reshape(resident_rows, hidden_width).astype(jnp.bfloat16)
    return (seq_in + jnp.dot(attn_rows, w_out, preferred_element_type=jnp.float32)).astype(
        jnp.bfloat16
    )


def solution(mesh):
    in_specs = (
        P(("tile", "seq"), None),
        P(),
        P(None, "tile"),
        P(None, "tile"),
        P("tile", None),
        P(),
        P(),
        P(),
        P(("tile", "seq")),
        P(None, ("tile", "seq")),
        P(),
        P(),
        P(),
        P(),
    )
    out_specs = P(("tile", "seq"), None)
    return jax.shard_map(body, mesh=mesh, in_specs=in_specs, out_specs=out_specs, check_vma=False)
```

profile of v0, /device:TPU:1, one launch (start us, length us, event | category | flops | bytes accessed | tf_op | source)
XLA Modules:
  0.0 357.2 jit_solution(11485548192163310712)
XLA Ops:
  6.5 1.3 convert_reduce_fusion
  7.8 1.2 fusion.31
  9.1 2.0 fusion.33
  11.2 64.7 %all-gather.4.cloned.1.call-done = bf16[2048,1536]{1,0:T(8,128)(2,1)} async-done(((bf16[128,1536]{1,0:T(8,128)(2,1)}), bf16[2048,1536]{1,0:T(8,128)(2,1)}) %all-gather.4.cloned.1.call-update) | async-done | bytes 6291472 | tf_op jit(solution)/shard_map/all_gather | solution.py:64
  75.9 6.1 %fusion.70 = f32[2048,256]{1,0:T(8,128)} fusion(bf16[2048,1536]{1,0:T(8,128)(2,1)} %all-gather.4.cloned.1.call-done, bf16[1536,256]{1,0:T(8,128)(2,1)} %param.16), kind=kOutput, calls=%fused_computation.112 | convolution fusion | flops 1610612736 | bytes 9175040 | tf_op jit(solution)/shard_map/dot_general | solution.py:65
  82.0 14.6 %fusion.7 = f32[2048,1536]{1,0:T(8,128)} fusion(bf16[256,1536]{1,0:T(8,128)(2,1)} %param.18, bf16[2048,1536]{1,0:T(8,128)(2,1)} %all-gather.4.cloned.1.call-done, bf16[1536,256]{1,0:T(8,128)(2,1)} %param.17, f32[2048,256]{1,0:T(8,128)} %fusion.70), kind=kOutput, calls=%fused_computation.14 | convolution fusion | flops 3224371200 | bytes 22544384 | tf_op jit(solution)/shard_map/dot_general | solution.py:69
  96.6 0.8 slice_bitcast_fusion.1
  97.4 1.2 pad_add_fusion
  98.6 1.4 copy.75
  100.0 0.7 and_select_fusion.1
  100.9 1.2 compare_select_fusion.4
  102.0 1.8 scatter_custom_fusion
  103.8 8.3 %all-to-all-start = ((s32[128,2,3]{2,1,0:T(2,128)}), s32[128,2,3]{2,1,0:T(2,128)}, u32[]{:S(2)}, u32[]{:S(2)}) async-start(s32[128,2,3]{2,1,0:T(2,128)} %bitcast.76), calls=%async_computation | async-start | bytes 262144 | tf_op jit(solution)/shard_map/all_to_all | solution.py:98
  112.8 9.2 %all-to-all-done = s32[128,2,3]{2,1,0:T(2,128)} async-done(((s32[128,2,3]{2,1,0:T(2,128)}), s32[128,2,3]{2,1,0:T(2,128)}, u32[]{:S(2)}, u32[]{:S(2)}) %all-to-all-start) | async-done | bytes 3104 | tf_op jit(solution)/shard_map/all_to_all | solution.py:98
  122.0 1.5 copy.93
  123.5 68.9 %reduce-scatter.2.cloned.1.call-done = f32[128,1536]{1,0:T(8,128)} async-done(((f32[2048,1536]{1,0:T(8,128)}), f32[128,1536]{1,0:T(8,128)}) %reduce-scatter.2.cloned.1.call-update) | async-done | bytes 786448 | tf_op jit(solution)/shard_map/reduce_scatter | solution.py:68
  192.4 1.5 fusion.39
  193.9 1.5 multiply_reduce_fusion.1
  195.4 2.9 convolution_convert_fusion.1
  198.3 2.3 scatter_custom_fusion.1
  200.6 1.9 reshape.194
  202.5 7.8 %all-to-all-start.1 = ((bf16[128,2,768]{2,1,0:T(2,128)(2,1)}), bf16[128,2,768]{2,1,0:T(2,128)(2,1)}, u32[]{:S(2)}, u32[]{:S(2)}) async-start(bf16[128,2,768]{2,1,0:T(2,128)(2,1)} %reshape.194), calls=%async_computation.2 | async-start | bytes 786432 | tf_op jit(solution)/shard_map/all_to_all | solution.py:91
  210.3 0.6 compare_select_fusion
  211.0 2.2 scatter_custom_fusion.3
  213.2 1.1 fusion.52
  214.3 2.5 multiply_sine_fusion.1
  216.7 5.6 %all-to-all-done.1 = bf16[128,2,768]{2,1,0:T(2,128)(2,1)} async-done(((bf16[128,2,768]{2,1,0:T(2,128)(2,1)}), bf16[128,2,768]{2,1,0:T(2,128)(2,1)}, u32[]{:S(2)}, u32[]{:S(2)}) %all-to-all-start.1) | async-done | bytes 393248 | tf_op jit(solution)/shard_map/all_to_all | solution.py:91
  222.3 1.9 reshape.224
  224.2 2.7 scatter_custom_fusion.2
  226.9 1.4 fusion.66
  228.6 0.7 convolution_convert_fusion
  229.3 0.8 copy-done.7
  230.1 0.8 slice.54
  231.0 2.6 reshape.199
  233.5 2.2 select_reduce_fusion
  235.8 1.6 reshape.200
  237.4 0.7 copy.80
  238.1 0.7 broadcast_in_dim.118
  238.7 0.7 broadcast_in_dim.119
  239.4 1.6 slice.53
  241.1 1.8 copy.81
  242.8 2.1 reshape.198
  244.9 1.9 select_reduce_fusion.1
  246.8 8.7 %all-gather.6.cloned.1.call-done = bf16[1024,1536]{1,0:T(8,128)(2,1)} async-done(((bf16[128,1536]{1,0:T(8,128)(2,1)}), bf16[1024,1536]{1,0:T(8,128)(2,1)}) %all-gather.6.cloned.1.call-update) | async-done | bytes 3145744 | tf_op jit(solution)/shard_map/all_gather | solution.py:123
  255.4 3.8 %fusion.68 = (bf16[1024,768]{1,0:T(8,128)(2,1)}, bf16[1024,768]{1,0:T(8,128)(2,1)}) fusion(bf16[1024,1536]{1,0:T(8,128)(2,1)} %all-gather.6.cloned.1.call-done), kind=kLoop, calls=%fused_computation.110 | loop fusion | bytes 6291456 | tf_op jit(solution)/shard_map/slice | solution.py:126
  259.2 2.6 copy.82
  261.9 2.6 copy.85
  264.5 2.6 multiply_reduce_fusion
  267.1 2.7 copy-done.1
  269.8 1.9 fusion.1
  271.7 52.7 %all-gather.8.cloned.1.call-done = bf16[1024,1536]{1,0:T(8,128)(2,1)} async-done(((bf16[8,1536]{1,0:T(8,128)(2,1)}), bf16[1024,1536]{1,0:T(8,128)(2,1)}) %all-gather.8.cloned.1.call-update) | async-done | bytes 3145744 | tf_op jit(solution)/shard_map/all_gather | solution.py:143
  324.3 3.8 %fusion.67 = (bf16[1024,768]{1,0:T(8,128)(2,1)}, bf16[1024,768]{1,0:T(8,128)(2,1)}) fusion(bf16[1024,1536]{1,0:T(8,128)(2,1)} %all-gather.8.cloned.1.call-done), kind=kLoop, calls=%fused_computation.109 | loop fusion | bytes 6291456 | tf_op jit(solution)/shard_map/slice | solution.py:146
  328.1 2.6 copy.83
  330.7 1.8 fusion.69
  332.5 0.7 copy-done.6
  334.1 0.7 sub.77
  334.8 1.5 sub.78
  336.2 2.6 copy.86
  338.8 2.1 fusion.15
  340.9 1.0 broadcast_in_dim.128
  341.9 2.1 copy.89
  344.0 0.7 broadcast_subtract_fusion
  344.8 4.8 %fusion.26 = bf16[128,12,64]{0,2,1:T(8,128)(2,1)S(1)} fusion(bf16[1024,12,64]{0,2,1:T(8,128)(2,1)} %bitcast.74, f32[12,128,1024]{2,1,0:T(8,128)} %copy-done.1, f32[12,128]{1,0:T(8,128)S(1)} %get-tuple-element.23, f32[128,12,64]{0,2,1:T(8,128)} %copy.89, f32[128,12]{0,1:T(8,128)S(1)} %get-tuple-element.8, f32[128,12]{0,1:T(8,128)} %bitcast.79, ...), kind=kOutput, calls=%fused_computation.33 | convolution fusion | flops 206635008 | bytes 8480256 | tf_op jit(solution)/shard_map/hqk,khd->qhd/dot_general | solution.py:37
  349.6 1.0 fusion.14
  (45 shorter events, 2.0 us)
Async XLA Ops:
  6.5 222.0 %copy-start = (bf16[768,2304]{1,0:T(8,128)(2,1)S(1)}, bf16[768,2304]{1,0:T(8,128)(2,1)}, u32[]{:S(2)}) copy-start(bf16[768,2304]{1,0:T(8,128)(2,1)} %param.25) | copy-start | bytes 10616836
  6.5 69.4 %all-gather.4.cloned.1.call-start = ((), (), s32[]{:S(2)}) async-start(), calls=%async_computation.3 | async-start | bytes 6684672 | tf_op jit(solution)/shard_map/all_gather | solution.py:64
  11.1 181.2 %reduce-scatter.2.cloned.1.call-start = ((), (), s32[]{:S(2)}) async-start(), calls=%async_computation.4 | async-start | bytes 13369344 | tf_op jit(solution)/shard_map/reduce_scatter | solution.py:68
  96.6 95.8 %copy-start.9 = (f32[1536]{0:T(1024)S(1)}, f32[1536]{0:T(1024)}, u32[]{:S(2)}) copy-start(f32[1536]{0:T(1024)} %param.19) | copy-start | bytes 18436
  96.6 98.8 %copy-start.11 = (f32[1536]{0:T(1024)S(1)}, f32[1536]{0:T(1024)}, u32[]{:S(2)}) copy-start(f32[1536]{0:T(1024)} %param.20) | copy-start | bytes 18436
  103.8 18.1 %all-to-all-start = ((s32[128,2,3]{2,1,0:T(2,128)}), s32[128,2,3]{2,1,0:T(2,128)}, u32[]{:S(2)}, u32[]{:S(2)}) async-start(s32[128,2,3]{2,1,0:T(2,128)} %bitcast.76), calls=%async_computation | async-start | bytes 262144 | tf_op jit(solution)/shard_map/all_to_all | solution.py:98
  192.4 3.0 copy-start.2
  192.4 3.0 copy-start.3
  200.6 28.0 %copy-start.12 = (f32[768]{0:T(1024)S(1)}, f32[768]{0:T(1024)}, u32[]{:S(2)}) copy-start(f32[768]{0:T(1024)} %param.24) | copy-start | bytes 9220
  202.5 19.8 %all-to-all-start.1 = ((bf16[128,2,768]{2,1,0:T(2,128)(2,1)}), bf16[128,2,768]{2,1,0:T(2,128)(2,1)}, u32[]{:S(2)}, u32[]{:S(2)}) async-start(bf16[128,2,768]{2,1,0:T(2,128)(2,1)} %reshape.194), calls=%async_computation.2 | async-start | bytes 786432 | tf_op jit(solution)/shard_map/all_to_all | solution.py:91
  210.3 45.2 %all-gather.6.cloned.1.call-start = ((), (), s32[]{:S(2)}) async-start(), calls=%async_computation.5 | async-start | bytes 3538944 | tf_op jit(solution)/shard_map/all_gather | solution.py:123
  228.3 0.9 copy-start.4
  228.5 2.4 copy-start.13
  229.2 0.8 copy-start.7
  230.9 93.4 %all-gather.8.cloned.1.call-start = ((), (), s32[]{:S(2)}) async-start(), calls=%async_computation.6 | async-start | bytes 3170304 | tf_op jit(solution)/shard_map/all_gather | solution.py:143
  267.1 2.7 copy-start.1
  332.5 0.7 copy-start.6
  333.5 0.6 copy-start.10
  344.8 4.8 %copy-start.5 = (f32[128,768]{1,0:T(8,128)S(1)}, f32[128,768]{1,0:T(8,128)}, u32[]{:S(2)}) copy-start(f32[128,768]{1,0:T(8,128)} %copy-done.4) | copy-start | bytes 1179652
  344.8 4.8 %copy-start.8 = (bf16[768,768]{1,0:T(8,128)(2,1)S(1)}, bf16[768,768]{1,0:T(8,128)(2,1)}, u32[]{:S(2)}) copy-start(bf16[768,768]{1,0:T(8,128)(2,1)} %param.27) | copy-start | bytes 3538948
Sparse Core Ops, SparseCore 0:
  11.3 64.6 all-gather.3
  96.7 95.5 reduce-scatter.1
  231.0 24.3 all-gather.5
  258.4 65.8 all-gather.7
where the time goes:
time: 358 us; the launch traced here: 357 us
  waiting for transfers between devices  210 us (59%)
  local copies, waits for them, and re-layouts  56.9 us (16%)
  matrix products  36.7 us (10%)
  other arithmetic  24.2 us (7%)
  starting transfers between devices  16.2 us (5%)
  between operations  13.4 us (4%)
    reduce_scatter x1, waiting for transfers between devices, body(): lax.psum_scatter(jnp.dot(hidden, w_down, preferred_element_type=jnp.float...  68.9 us
    all_gather x1, waiting for transfers between devices, body(): shard_rows = lax.all_gather(normed, 'tile', axis=0, tiled=True)  64.7 us
    all_gather x1, waiting for transfers between devices, body(): lax.all_gather(select(keys_values, 2), ('tile', 'seq'), axis=0, tiled=True)  52.7 us
    dot_general x1, matrix products, body(): jnp.dot(hidden, w_down, preferred_element_type=jnp.float32)  14.6 us
    all_to_all x1, waiting for transfers between devices, body(): lax.all_to_all(meta_table.reshape(devices, capacity, 3), ('tile', 'seq'),...  9.2 us
    all_gather x1, waiting for transfers between devices, body(): segment_kv = lax.all_gather(keys_values, 'seq', axis=0, tiled=True)  8.69 us
    all_to_all x1, starting transfers between devices, body(): lax.all_to_all(meta_table.reshape(devices, capacity, 3), ('tile', 'seq'),...  8.32 us
    all_to_all x1, starting transfers between devices, body(): lax.all_to_all(payload.reshape(devices, capacity, hidden_width), ('tile',...  7.79 us
  transfers between devices with their start and end apart: 6, of which 6 were waited for; matrix products, arithmetic and copies ran while one was open for 13% of the time, Pallas kernels for 0%

commit v1 on v0

--- a/solution.py
+++ b/solution.py
@@ -6,6 +6,28 @@
 HEAD_COUNT = 12
 HEAD_WIDTH = 64
 SEGMENT_SPACING = 16
+
+
+def remake_routes_all(message, which_dim):
+    carry, met_up, tile_out = (
+        lax.axis_size("seq"),
+        lax.axis_index("seq"),
+        message.shape[which_dim],
+    )
+    rows = list(map(lambda to_i: (to_i, (to_i + 1) % carry), range(carry)))
+    finding = jnp.zeros(
+        (*message.shape[:which_dim], carry * tile_out, *message.shape[which_dim + 1 :]),
+        message.dtype,
+    )
+    everything = message
+    for j in range(carry):
+        left_arr = (met_up - j) % carry
+        finding = lax.dynamic_update_slice_in_dim(
+            finding, everything, left_arr * tile_out, axis=which_dim
+        )
+        if j < carry - 1:
+            everything = lax.ppermute(everything, "seq", rows)
+    return finding
 
 
 def layer_norm(sender_rows, gain):
@@ -120,7 +142,7 @@
     qkv = jnp.dot(normed_seq, w_qkv, preferred_element_type=jnp.float32).astype(jnp.bfloat16)
     queries = qkv[:, :hidden_width]
     keys_values = qkv[:, hidden_width:]
-    segment_kv = lax.all_gather(keys_values, "seq", axis=0, tiled=True)
+    segment_kv = remake_routes_all(keys_values, 0)
     near_out, nearby_logsumexp = attend(
         queries.reshape(resident_rows, HEAD_COUNT, HEAD_WIDTH),
         segment_kv[:, :hidden_width].reshape(-1, HEAD_COUNT, HEAD_WIDTH),

time: 358 us -> 328 us (0.916)
  the two profiles are of different devices: /device:TPU:1 before, /device:TPU:0 now
where the time goes in v1:
time: 328 us; the launch traced here: 327 us
  waiting for transfers between devices  201 us (61%)
  local copies, waits for them, and re-layouts  44 us (13%)
  matrix products  34.1 us (10%)
  other arithmetic  17.4 us (5%)
  starting transfers between devices  17 us (5%)
  between operations  13.5 us (4%)
    reduce_scatter x1, waiting for transfers between devices, body(): lax.psum_scatter(jnp.dot(hidden, w_down, preferred_element_type=jnp.float...  73.1 us
    all_gather x1, waiting for transfers between devices, body(): shard_rows = lax.all_gather(normed, 'tile', axis=0, tiled=True)  64 us
    ppermute x7, waiting for transfers between devices, remake_routes_all(): everything = lax.ppermute(everything, 'seq', rows)  50.4 us
    dot_general x1, matrix products, body(): jnp.dot(hidden, w_down, preferred_element_type=jnp.float32)  14.7 us
    all_to_all x1, starting transfers between devices, body(): lax.all_to_all(meta_table.reshape(devices, capacity, 3), ('tile', 'seq'),...  8.79 us
    ppermute x7, local copies, waits for them, and re-layouts, remake_routes_all(): everything = lax.ppermute(everything, 'seq', rows)  8.51 us
    all_to_all x1, waiting for transfers between devices, body(): lax.all_to_all(meta_table.reshape(devices, capacity, 3), ('tile', 'seq'),...  8.07 us
    all_to_all x1, starting transfers between devices, body(): lax.all_to_all(payload.reshape(devices, capacity, hidden_width), ('tile',...  8.05 us
  transfers between devices with their start and end apart: 12, of which 11 were waited for; matrix products, arithmetic and copies ran while one was open for 9% of the time, Pallas kernels for 0%

profile of v1, /device:TPU:0, one launch (start us, length us, event | category | flops | bytes accessed | tf_op | source)
XLA Modules:
  0.0 327.1 jit_solution(11525024215987923628)
XLA Ops:
  6.5 1.3 convert_reduce_fusion
  7.8 1.2 fusion.31
  9.1 2.0 fusion.33
  11.2 64.0 %all-gather.3.cloned.1.call-done = bf16[2048,1536]{1,0:T(8,128)(2,1)} async-done(((bf16[128,1536]{1,0:T(8,128)(2,1)}), bf16[2048,1536]{1,0:T(8,128)(2,1)}) %all-gather.3.cloned.1.call-update) | async-done | bytes 6291472 | tf_op jit(solution)/shard_map/all_gather | solution.py:86
  75.2 6.0 %fusion.70 = f32[2048,256]{1,0:T(8,128)} fusion(bf16[2048,1536]{1,0:T(8,128)(2,1)} %all-gather.3.cloned.1.call-done, bf16[1536,256]{1,0:T(8,128)(2,1)} %param.16), kind=kOutput, calls=%fused_computation.120 | convolution fusion | flops 1610612736 | bytes 9175040 | tf_op jit(solution)/shard_map/dot_general | solution.py:87
  81.2 14.7 %fusion.7 = f32[2048,1536]{1,0:T(8,128)} fusion(bf16[256,1536]{1,0:T(8,128)(2,1)} %param.18, bf16[2048,1536]{1,0:T(8,128)(2,1)} %all-gather.3.cloned.1.call-done, bf16[1536,256]{1,0:T(8,128)(2,1)} %param.17, f32[2048,256]{1,0:T(8,128)} %fusion.70), kind=kOutput, calls=%fused_computation.14 | convolution fusion | flops 3224371200 | bytes 22544384 | tf_op jit(solution)/shard_map/dot_general | solution.py:91
  95.9 0.6 copy-done.16
  96.6 0.7 copy.105
  97.5 1.8 scatter_custom_fusion
  99.3 8.8 %all-to-all-start = ((s32[128,2,3]{2,1,0:T(2,128)}), s32[128,2,3]{2,1,0:T(2,128)}, u32[]{:S(2)}, u32[]{:S(2)}) async-start(s32[128,2,3]{2,1,0:T(2,128)} %bitcast.76), calls=%async_computation | async-start | bytes 262144 | tf_op jit(solution)/shard_map/all_to_all | solution.py:120
  108.1 0.7 iota_compare_fusion.1
  108.8 0.6 negate_power_fusion
  109.4 8.1 %all-to-all-done = s32[128,2,3]{2,1,0:T(2,128)} async-done(((s32[128,2,3]{2,1,0:T(2,128)}), s32[128,2,3]{2,1,0:T(2,128)}, u32[]{:S(2)}, u32[]{:S(2)}) %all-to-all-start) | async-done | bytes 3104 | tf_op jit(solution)/shard_map/all_to_all | solution.py:120
  117.4 1.0 copy.129
  118.4 73.1 %reduce-scatter.2.cloned.1.call-done = f32[128,1536]{1,0:T(8,128)} async-done(((f32[2048,1536]{1,0:T(8,128)}), f32[128,1536]{1,0:T(8,128)}) %reduce-scatter.2.cloned.1.call-update) | async-done | bytes 786448 | tf_op jit(solution)/shard_map/reduce_scatter | solution.py:90
  191.6 1.4 fusion.39
  193.0 1.5 multiply_reduce_fusion.1
  194.5 3.3 %convolution_convert_fusion.1 = bf16[128,768]{1,0:T(8,128)(2,1)} fusion(bf16[1536,768]{1,0:T(8,128)(2,1)} %param.21, f32[1536]{0:T(1024)} %param.20, f32[128]{0:T(128)S(1)} %add_rsqrt_fusion.1, f32[128]{0:T(128)S(1)} %broadcast_multiply_fusion.1, bf16[128,1536]{1,0:T(8,128)(2,1)} %param.14, f32[128,1536]{1,0:T(8,128)} %reduce-scatter.2.cloned.1.call-done, ...), kind=kOutput, calls=%fused_computation.25 | convolution fusion | flops 303464448 | bytes 3748864 | tf_op jit(solution)/shard_map/dot_general | solution.py:98
  197.8 2.3 scatter_custom_fusion.1
  200.0 1.9 reshape.194
  201.9 8.0 %all-to-all-start.1 = ((bf16[128,2,768]{2,1,0:T(2,128)(2,1)}), bf16[128,2,768]{2,1,0:T(2,128)(2,1)}, u32[]{:S(2)}, u32[]{:S(2)}) async-start(bf16[128,2,768]{2,1,0:T(2,128)(2,1)} %reshape.194), calls=%async_computation.2 | async-start | bytes 786432 | tf_op jit(solution)/shard_map/all_to_all | solution.py:113
  210.6 2.2 scatter_custom_fusion.3
  212.8 1.1 fusion.52
  213.9 2.5 multiply_sine_fusion.1
  216.3 5.4 %all-to-all-done.1 = bf16[128,2,768]{2,1,0:T(2,128)(2,1)} async-done(((bf16[128,2,768]{2,1,0:T(2,128)(2,1)}), bf16[128,2,768]{2,1,0:T(2,128)(2,1)}, u32[]{:S(2)}, u32[]{:S(2)}) %all-to-all-start.1) | async-done | bytes 393248 | tf_op jit(solution)/shard_map/all_to_all | solution.py:113
  221.7 1.9 reshape.224
  223.6 2.7 scatter_custom_fusion.2
  226.3 1.4 fusion.66
  228.5 0.7 convolution_convert_fusion
  229.2 0.8 copy-done.5
  230.0 0.9 reshape.199
  231.3 0.7 reshape.200
  232.1 8.4 %collective-permute-done = bf16[128,1536]{1,0:T(8,128)(2,1)S(1)} collective-permute-done((bf16[128,1536]{1,0:T(8,128)(2,1)S(1)}, bf16[128,1536]{1,0:T(8,128)(2,1)S(1)}, u32[]{:S(2)}, u32[]{:S(2)}) %collective-permute-start) | collective-permute-done | bytes 393248 | tf_op jit(solution)/shard_map/ppermute | solution.py:29
  240.5 8.5 %collective-permute-done.1 = bf16[128,1536]{1,0:T(8,128)(2,1)S(1)} collective-permute-done((bf16[128,1536]{1,0:T(8,128)(2,1)S(1)}, bf16[128,1536]{1,0:T(8,128)(2,1)S(1)}, u32[]{:S(2)}, u32[]{:S(2)}) %collective-permute-start.1) | collective-permute-done | bytes 393248 | tf_op jit(solution)/shard_map/ppermute | solution.py:29
  249.0 8.5 %collective-permute-done.2 = bf16[128,1536]{1,0:T(8,128)(2,1)} collective-permute-done((bf16[128,1536]{1,0:T(8,128)(2,1)S(1)}, bf16[128,1536]{1,0:T(8,128)(2,1)}, u32[]{:S(2)}, u32[]{:S(2)}) %collective-permute-start.2) | collective-permute-done | bytes 393248 | tf_op jit(solution)/shard_map/ppermute | solution.py:29
  257.6 0.7 broadcast_in_dim.122
  258.6 0.9 slice.53
  259.5 0.8 copy.111
  260.7 0.8 select_reduce_fusion.1
  262.0 1.2 copy.113
  263.2 3.4 %collective-permute-done.3 = bf16[128,1536]{1,0:T(8,128)(2,1)} collective-permute-done((bf16[128,1536]{1,0:T(8,128)(2,1)}, bf16[128,1536]{1,0:T(8,128)(2,1)}, u32[]{:S(2)}, u32[]{:S(2)}) %collective-permute-start.3) | collective-permute-done | bytes 393248 | tf_op jit(solution)/shard_map/ppermute | solution.py:29
  266.7 1.2 copy.114
  268.1 1.2 copy.115
  269.3 6.2 %collective-permute-done.4 = bf16[128,1536]{1,0:T(8,128)(2,1)} collective-permute-done((bf16[128,1536]{1,0:T(8,128)(2,1)}, bf16[128,1536]{1,0:T(8,128)(2,1)}, u32[]{:S(2)}, u32[]{:S(2)}) %collective-permute-start.4) | collective-permute-done | bytes 393248 | tf_op jit(solution)/shard_map/ppermute | solution.py:29
  275.6 1.2 copy.116
  277.0 1.2 copy.117
  278.2 7.6 %collective-permute-done.5 = bf16[128,1536]{1,0:T(8,128)(2,1)} collective-permute-done((bf16[128,1536]{1,0:T(8,128)(2,1)}, bf16[128,1536]{1,0:T(8,128)(2,1)}, u32[]{:S(2)}, u32[]{:S(2)}) %collective-permute-start.5) | collective-permute-done | bytes 393248 | tf_op jit(solution)/shard_map/ppermute | solution.py:29
  286.0 1.2 copy.118
  287.3 7.9 %collective-permute-done.6 = bf16[128,1536]{1,0:T(8,128)(2,1)} collective-permute-done((bf16[128,1536]{1,0:T(8,128)(2,1)}, bf16[128,1536]{1,0:T(8,128)(2,1)}, u32[]{:S(2)}, u32[]{:S(2)}) %collective-permute-start.6) | collective-permute-done | bytes 393248 | tf_op jit(solution)/shard_map/ppermute | solution.py:29
  295.2 1.2 copy.119
  296.6 1.5 fusion.68
  298.1 1.1 multiply_reduce_fusion
  299.2 2.7 copy-done.2
  301.9 1.9 fusion.1
  303.8 3.2 fusion.67
  307.0 1.7 copy.120
  308.7 1.2 fusion.69
  310.1 0.6 copy-done.11
  310.7 0.7 sub.106
  311.4 0.7 copy.122
  312.2 1.3 fusion.15
  313.6 1.0 copy.125
  314.6 4.8 %fusion.26 = bf16[128,12,64]{0,2,1:T(8,128)(2,1)S(1)} fusion(bf16[1024,12,64]{0,2,1:T(8,128)(2,1)} %bitcast.74, f32[12,128,1024]{2,1,0:T(8,128)} %copy-done.2, f32[12,128]{1,0:T(8,128)S(1)} %get-tuple-element.23, f32[128,12,64]{0,2,1:T(8,128)} %copy.125, f32[128,12]{0,1:T(8,128)S(1)} %get-tuple-element.8, f32[128,12]{0,1:T(8,128)} %bitcast.79, ...), kind=kOutput, calls=%fused_computation.33 | convolution fusion | flops 206635008 | bytes 8480256 | tf_op jit(solution)/shard_map/hqk,khd->qhd/dot_general | solution.py:59
  319.5 1.0 fusion.14
  (83 shorter events, 4.7 us)
Async XLA Ops:
  6.5 222.0 %copy-start = (bf16[768,2304]{1,0:T(8,128)(2,1)S(1)}, bf16[768,2304]{1,0:T(8,128)(2,1)}, u32[]{:S(2)}) copy-start(bf16[768,2304]{1,0:T(8,128)(2,1)} %param.25) | copy-start | bytes 10616836
  6.5 68.6 %all-gather.3.cloned.1.call-start = ((), (), s32[]{:S(2)}) async-start(), calls=%async_computation.3 | async-start | bytes 6684672 | tf_op jit(solution)/shard_map/all_gather | solution.py:86
  11.1 180.4 %reduce-scatter.2.cloned.1.call-start = ((), (), s32[]{:S(2)}) async-start(), calls=%async_computation.4 | async-start | bytes 13369344 | tf_op jit(solution)/shard_map/reduce_scatter | solution.py:90
  95.9 0.7 copy-start.16
  95.9 0.7 copy-start.18
  95.9 95.7 %copy-start.10 = (f32[1536]{0:T(1024)S(1)}, f32[1536]{0:T(1024)}, u32[]{:S(2)}) copy-start(f32[1536]{0:T(1024)} %param.19) | copy-start | bytes 18436
  97.5 1.8 copy-start.19
  99.3 18.1 %all-to-all-start = ((s32[128,2,3]{2,1,0:T(2,128)}), s32[128,2,3]{2,1,0:T(2,128)}, u32[]{:S(2)}, u32[]{:S(2)}) async-start(s32[128,2,3]{2,1,0:T(2,128)} %bitcast.76), calls=%async_computation | async-start | bytes 262144 | tf_op jit(solution)/shard_map/all_to_all | solution.py:120
  197.8 30.8 %copy-start.15 = (f32[768]{0:T(1024)S(1)}, f32[768]{0:T(1024)}, u32[]{:S(2)}) copy-start(f32[768]{0:T(1024)} %param.24) | copy-start | bytes 9220
  201.9 19.8 %all-to-all-start.1 = ((bf16[128,2,768]{2,1,0:T(2,128)(2,1)}), bf16[128,2,768]{2,1,0:T(2,128)(2,1)}, u32[]{:S(2)}, u32[]{:S(2)}) async-start(bf16[128,2,768]{2,1,0:T(2,128)(2,1)} %reshape.194), calls=%async_computation.2 | async-start | bytes 786432 | tf_op jit(solution)/shard_map/all_to_all | solution.py:113
  210.0 93.8 %all-gather.5.cloned.1.call-start = ((), (), s32[]{:S(2)}) async-start(), calls=%async_computation.5 | async-start | bytes 3170304 | tf_op jit(solution)/shard_map/all_gather | solution.py:165
  210.0 0.5 copy-start.17
  227.7 0.8 copy-start.3
  229.2 0.8 copy-start.5
  232.1 8.4 %collective-permute-start = (bf16[128,1536]{1,0:T(8,128)(2,1)S(1)}, bf16[128,1536]{1,0:T(8,128)(2,1)S(1)}, u32[]{:S(2)}, u32[]{:S(2)}) collective-permute-start(bf16[128,1536]{1,0:T(8,128)(2,1)S(1)} %slice.54), channel_id=1, source_target_pairs={{0,1},{1,2},{2,3},{3,4},{4,5},{5,6},{6,7},{7,0},{8,9},{9,10},{10,1... | collective-permute-start | bytes 1179656 | tf_op jit(solution)/shard_map/ppermute | solution.py:29
  240.5 17.8 %copy-start.9 = (bf16[128,1536]{1,0:T(8,128)(2,1)}, bf16[128,1536]{1,0:T(8,128)(2,1)S(1)}, u32[]{:S(2)}) copy-start(bf16[128,1536]{1,0:T(8,128)(2,1)S(1)} %collective-permute-done) | copy-start | bytes 1179652
  240.5 8.5 %collective-permute-start.1 = (bf16[128,1536]{1,0:T(8,128)(2,1)S(1)}, bf16[128,1536]{1,0:T(8,128)(2,1)S(1)}, u32[]{:S(2)}, u32[]{:S(2)}) collective-permute-start(bf16[128,1536]{1,0:T(8,128)(2,1)S(1)} %collective-permute-done), channel_id=1, source_target_pairs={{0,1},{1,2},{2,3},{3,4},{4,5},{5,6},{6,7},{7,0},{8,9},{9,10},{10,1... | collective-permute-start | bytes 1179656 | tf_op jit(solution)/shard_map/ppermute | solution.py:29
  249.0 10.5 %copy-start.8 = (bf16[128,1536]{1,0:T(8,128)(2,1)}, bf16[128,1536]{1,0:T(8,128)(2,1)S(1)}, u32[]{:S(2)}) copy-start(bf16[128,1536]{1,0:T(8,128)(2,1)S(1)} %collective-permute-done.1) | copy-start | bytes 1179652
  249.0 8.5 %collective-permute-start.2 = (bf16[128,1536]{1,0:T(8,128)(2,1)S(1)}, bf16[128,1536]{1,0:T(8,128)(2,1)}, u32[]{:S(2)}, u32[]{:S(2)}) collective-permute-start(bf16[128,1536]{1,0:T(8,128)(2,1)S(1)} %collective-permute-done.1), channel_id=1, source_target_pairs={{0,1},{1,2},{2,3},{3,4},{4,5},{5,6},{6,7},{7,0},{8,9},{9,10},{10,1... | collective-permute-start | bytes 1179656 | tf_op jit(solution)/shard_map/ppermute | solution.py:29
  257.5 9.1 %collective-permute-start.3 = (bf16[128,1536]{1,0:T(8,128)(2,1)}, bf16[128,1536]{1,0:T(8,128)(2,1)}, u32[]{:S(2)}, u32[]{:S(2)}) collective-permute-start(bf16[128,1536]{1,0:T(8,128)(2,1)} %collective-permute-done.2), channel_id=1, source_target_pairs={{0,1},{1,2},{2,3},{3,4},{4,5},{5,6},{6,7},{7,0},{8,9},{9,10},{10,1... | collective-permute-start | bytes 1179656 | tf_op jit(solution)/shard_map/ppermute | solution.py:29
  266.6 8.9 %collective-permute-start.4 = (bf16[128,1536]{1,0:T(8,128)(2,1)}, bf16[128,1536]{1,0:T(8,128)(2,1)}, u32[]{:S(2)}, u32[]{:S(2)}) collective-permute-start(bf16[128,1536]{1,0:T(8,128)(2,1)} %collective-permute-done.3), channel_id=1, source_target_pairs={{0,1},{1,2},{2,3},{3,4},{4,5},{5,6},{6,7},{7,0},{8,9},{9,10},{10,1... | collective-permute-start | bytes 1179656 | tf_op jit(solution)/shard_map/ppermute | solution.py:29
  275.5 10.3 %collective-permute-start.5 = (bf16[128,1536]{1,0:T(8,128)(2,1)}, bf16[128,1536]{1,0:T(8,128)(2,1)}, u32[]{:S(2)}, u32[]{:S(2)}) collective-permute-start(bf16[128,1536]{1,0:T(8,128)(2,1)} %collective-permute-done.4), channel_id=1, source_target_pairs={{0,1},{1,2},{2,3},{3,4},{4,5},{5,6},{6,7},{7,0},{8,9},{9,10},{10,1... | collective-permute-start | bytes 1179656 | tf_op jit(solution)/shard_map/ppermute | solution.py:29
  285.8 9.4 %collective-permute-start.6 = (bf16[128,1536]{1,0:T(8,128)(2,1)}, bf16[128,1536]{1,0:T(8,128)(2,1)}, u32[]{:S(2)}, u32[]{:S(2)}) collective-permute-start(bf16[128,1536]{1,0:T(8,128)(2,1)} %collective-permute-done.5), channel_id=1, source_target_pairs={{0,1},{1,2},{2,3},{3,4},{4,5},{5,6},{6,7},{7,0},{8,9},{9,10},{10,1... | collective-permute-start | bytes 1179656 | tf_op jit(solution)/shard_map/ppermute | solution.py:29
  296.6 1.5 copy-start.7
  299.2 2.7 copy-start.2
  310.1 0.6 copy-start.11
  312.2 2.4 copy-start.12
  312.2 2.4 copy-start.13
  312.2 2.4 copy-start.14
  314.6 4.9 %copy-start.4 = (f32[128,768]{1,0:T(8,128)S(1)}, f32[128,768]{1,0:T(8,128)}, u32[]{:S(2)}) copy-start(f32[128,768]{1,0:T(8,128)} %copy-done.3) | copy-start | bytes 1179652
  314.6 4.9 %copy-start.6 = (bf16[768,768]{1,0:T(8,128)(2,1)S(1)}, bf16[768,768]{1,0:T(8,128)(2,1)}, u32[]{:S(2)}) copy-start(bf16[768,768]{1,0:T(8,128)(2,1)} %param.27) | copy-start | bytes 3538948
  314.6 5.9 %copy-start.1 = (bf16[768,2304]{1,0:T(8,128)(2,1)S(1)}, bf16[768,2304]{1,0:T(8,128)(2,1)}, u32[]{:S(2)}) copy-start(bf16[768,2304]{1,0:T(8,128)(2,1)} %param.25) | copy-start | bytes 10616836
Sparse Core Ops, SparseCore 0:
  11.3 63.8 all-gather.2
  96.0 95.4 reduce-scatter.1
  232.2 62.1 all-gather.4
